TPU v7x, 32 devices: a whole 2x2x4 slice. The times are simulated.
32 devices in a mesh: dp: 4 (over y, x), expert: 8 (over z, core).
Axes of the slice: x: 2, y: 2, z: 4, core: 2. Of those that a mesh axis runs over, the one named last changes fastest.
Arguments:
- block_input: bfloat16 [4096, 512], P(('dp', 'expert')), may hold values from -6 to 6
- cotangent: bfloat16 [4096, 512], P(('dp', 'expert')), may hold values from -6 to 6
- lengths: int32 [4, 6], P('dp'), may hold values from 1 to 512, 896 in all within a row
- run_loops: int32 [4096], P('dp'), may hold values from 1 to 3
- attn_routes: int32 [3, 4096, 4], P(None, 'dp'), may hold values from 0 to 7, all different within a row; in each aligned block of 1024 rows (0 to 1023, 1024 to 2047, ..., all dimensions but the last counted through in order) at most 640 rows name the same one
- ffn_routes: int32 [3, 4096, 2], P(None, 'dp'), may hold values from 0 to 7, all different within a row; in each aligned block of 1024 rows (0 to 1023, 1024 to 2047, ..., all dimensions but the last counted through in order) at most 320 rows name the same one
- shared_vectors: float32 [5, 512], replicated, as said below
- shared_moment: float32 [5, 512], replicated
- shared_second: float32 [5, 512], replicated, as said below
- key_value: float32 [512, 128], replicated, may hold values from -0.25 to 0.25
- kv_moment: float32 [512, 128], replicated, may hold values from -112 to 112
- kv_second: float32 [512, 128], replicated, may hold values from 358.4 to 1433.6
- router_weights: float32 [512, 16], replicated, may hold values from -0.15625 to 0.15625
- router_moment: float32 [512, 16], replicated, may hold values from -16 to 16
- router_second: float32 [512, 16], replicated, may hold values from 96.0512 to 387.072
- attn_weights: float32 [8, 512, 128], P('expert', 'dp')
- attn_moment: float32 [8, 512, 128], P('expert', 'dp')
- attn_second: float32 [8, 512, 128], P('expert', 'dp'), as said below
- up_weights: float32 [8, 512, 2048], P('expert', 'dp'), may hold values from -0.25 to 0.25
- up_moment: float32 [8, 512, 2048], P('expert', 'dp'), may hold values from -4 to 4
- up_second: float32 [8, 512, 2048], P('expert', 'dp'), may hold values from 0.25088 to 1.00352
- down_weights: float32 [8, 512, 2048], P('expert', 'dp'), may hold values from -0.125 to 0.125
- down_moment: float32 [8, 512, 2048], P('expert', 'dp'), may hold values from -8 to 8
- down_second: float32 [8, 512, 2048], P('expert', 'dp'), may hold values from 1.792 to 7.168
Outputs:
- output: float32 [4096, 512], P(('dp', 'expert'))
- input_grad: float32 [4096, 512], P(('dp', 'expert'))
- shared_new: float32 [5, 512], replicated
- shared_moment_new: float32 [5, 512], replicated
- shared_second_new: float32 [5, 512], replicated
- kv_new: float32 [512, 128], replicated
- kv_moment_new: float32 [512, 128], replicated
- kv_second_new: float32 [512, 128], replicated
- router_new: float32 [512, 16], replicated
- router_moment_new: float32 [512, 16], replicated
- router_second_new: float32 [512, 16], replicated
- attn_new: float32 [8, 512, 128], P('expert', 'dp')
- attn_moment_new: float32 [8, 512, 128], P('expert', 'dp')
- attn_second_new: float32 [8, 512, 128], P('expert', 'dp')
- attn_copy: bfloat16 [8, 512, 128], P('expert', 'dp')
- up_new: float32 [8, 512, 2048], P('expert', 'dp')
- up_moment_new: float32 [8, 512, 2048], P('expert', 'dp')
- up_second_new: float32 [8, 512, 2048], P('expert', 'dp')
- up_copy: bfloat16 [8, 512, 2048], P('expert', 'dp')
- down_new: float32 [8, 512, 2048], P('expert', 'dp')
- down_moment_new: float32 [8, 512, 2048], P('expert', 'dp')
- down_second_new: float32 [8, 512, 2048], P('expert', 'dp')
- down_copy: bfloat16 [8, 512, 2048], P('expert', 'dp')
Inputs may be any that keep to these rules, and one draw needn't show every extreme that they name: The lengths of one data device sum to 896; the remaining slots are padding. `attn_routes`: each row names 4 different experts; in each loop at most 640 rows of one data device name one expert, and that many do in some blocks. `ffn_routes`: each row names 2 different experts; in each loop at most 320 rows of one data device name one expert, and that many do in some blocks. `shared_vectors`: gains positive, biases and the halting weight of both signs. `shared_second`: Positive. `attn_second`: Positive.
All inputs are finite; a program needn't handle non-finite values.
Results may differ from a plain program's by a relative error of at most 0.025.
The roundings to bfloat16 on the way count: a program that leaves them out, or rounds other values in their place, can miss the bound.
Values may be sent and summed in bfloat16 or wider, within the bound.
A program may use at most 192 MiB of HBM per device.

v0:
```python
import functools
import math

import jax
import jax.numpy as jnp
from jax import lax
from jax.experimental import pallas as pl
from jax.experimental.pallas import tpu as pltpu
from jax.sharding import PartitionSpec as P

D = 512
HD = 64
FF = 2048
KATT = 4
KFF = 2
LOOPS = 3
STEP = 10
MAXLEN = 512
FILLED = 896

ln_eps = 1e-05
beta_one = 0.9
beta_two = 0.999
adam_eps = 1e-08
decay_rate = 0.01
masked_score = -1e30

F32 = jnp.float32
BF16 = jnp.bfloat16
MESH = pl.DeviceIdType.MESH
LANES = 128
RANK_LANE = 16
RUN_LANE = 17
SEG_LANE = 18
INFO = 32
TILE = 512
EXTRA = 16


def nn(left, right):
    return lax.dot_general(left, right, (((1,), (0,)), ((), ())), preferred_element_type=F32)


def nt(left, right):
    return lax.dot_general(left, right, (((1,), (1,)), ((), ())), preferred_element_type=F32)


def tn(left, right):
    return lax.dot_general(left, right, (((0,), (0,)), ((), ())), preferred_element_type=F32)


def normalise(values):
    centre = values - jnp.mean(values, axis=-1, keepdims=True)
    inverse = lax.rsqrt(jnp.mean(centre * centre, axis=-1, keepdims=True) + ln_eps)
    return centre * inverse, inverse


def norm_back(grad, unit, inverse, gain):
    scaled = grad * gain
    first = jnp.mean(scaled, axis=-1, keepdims=True)
    second = jnp.mean(scaled * unit, axis=-1, keepdims=True)
    return inverse * (scaled - first - unit * second)


def masked_softmax(logits, valid):
    top = jnp.max(jnp.where(valid, logits, masked_score), axis=-1, keepdims=True)
    powers = jnp.where(valid, jnp.exp(jnp.where(valid, logits - top, 0.0)), 0.0)
    return powers / jnp.maximum(jnp.sum(powers, axis=-1, keepdims=True), 0.5)


def adam_update(weight, moment, second, grad, rate, decay):
    moment_new = beta_one * moment + (1.0 - beta_one) * grad
    second_new = beta_two * second + (1.0 - beta_two) * grad * grad
    moment_hat = moment_new * (1.0 / (1.0 - beta_one**STEP))
    second_hat = second_new * (1.0 / (1.0 - beta_two**STEP))
    weight_new = weight - rate * (moment_hat / (jnp.sqrt(second_hat) + adam_eps) + decay * weight)
    return (weight_new, moment_new, second_new)


def block_kernel(
    n_exp,
    n_dp,
    n_act,
    cap,
    x_ref,
    cot_ref,
    len_ref,
    run_ref,
    ar_ref,
    fr_ref,
    vec_ref,
    kvw_ref,
    rw_ref,
    aw_ref,
    uw_hbm,
    dw_hbm,
    out_ref,
    xgrad_ref,
    ugrad_ref,
    dgrad_ref,
    agrad_ref,
    kvgrad_ref,
    rgrad_ref,
    vgrad_ref,
    meta_ref,
    rowm_ref,
    kvb,
    rb,
    w_all,
    up_w,
    down_w,
    up_acc,
    down_acc,
    attn_acc,
    small_acc,
    state,
    middle,
    normed_k,
    second_k,
    kv_k,
    q_k,
    o_k,
    p_k,
    ds_k,
    bias,
    mix,
    dga,
    dkv_t,
    dkv,
    gate_k,
    rows_all,
    wrow,
    gather_m,
    scatter_m,
    rows_k,
    hid,
    gprime,
    row_grads,
    part_k,
    fgate_k,
    chosen_k,
    ggrad,
    scaled_k,
    sgrad,
    carry,
    mgrad,
    total,
    total_two,
    pair_send,
    pair_recv,
    far_send,
    far_recv,
    pair_send_two,
    pair_recv_two,
    far_send_two,
    far_recv_two,
    dkv_send,
    dkv_recv,
    u_first,
    u_last,
    d_first,
    d_last,
    a_total,
    a_stage,
    a_recv,
    s_pair_send,
    s_pair_recv,
    s_far_send,
    s_far_recv,
    s_total,
    s_dp,
    s_all,
    in_sems,
    w_send,
    w_recv,
    uw_send,
    uw_recv,
    uw_send_two,
    dw_send,
    dw_recv,
    dw_send_two,
    ag_send,
    ag_recv,
    bg_send,
    bg_recv,
    fg_send,
    fg_recv,
    wg_send,
    wg_recv,
    sg_send,
    sg_recv,
    kg_send,
    kg_recv,
    rs_sems,
    rs_sems_two,
    s_sems,
    a_sems,
    dk_send,
    dk_recv,
    ug_send,
    ug_recv,
    ug_send_two,
    ug_recv_two,
    dg_send,
    dg_recv,
    dg_send_two,
    dg_recv_two,
    t_send,
    t_recv,
):
    me = lax.axis_index("expert")
    dp = lax.axis_index("dp")
    pairs = n_exp // 2
    core = lax.rem(me, 2)
    chip = lax.div(me, 2)
    sibling = 2 * chip + 1 - core
    n_low, n_high = dp_grid(n_dp)
    high = lax.div(dp, n_low)
    low = lax.rem(dp, n_low)
    own = x_ref.shape[0]
    width = x_ref.shape[1]
    slots = run_ref.shape[1]
    shard = aw_ref.shape[0]
    hidden_units = up_w.shape[1]
    tiles = hidden_units // TILE
    valid_rows = n_act * own
    window = min(n_act, MAXLEN // own + 1)
    keys = window * own
    win_at = jnp.clip(me - (window - 1), 0, n_act - window)
    scale = HD ** (-0.5)
    active = me < n_act
    last = LOOPS - 1

    def remote(src, dst, send, recv, **where):
        return pltpu.make_async_remote_copy(
            src_ref=src,
            dst_ref=dst,
            send_sem=send,
            recv_sem=recv,
            device_id=where,
            device_id_type=MESH,
        )

    def shard_rows(index, count=1):
        return pl.ds(pl.multiple_of(index * shard, shard), count * shard)

    def each_peer(body):
        def step(k, none):
            body(lax.rem(dp + k, n_dp))
            return none

        lax.fori_loop(1, n_dp, step, 0)

    def high_peers():
        return [lax.rem(high + k, n_high) for k in range(1, n_high)]

    def low_peers():
        return [lax.rem(low + k, n_low) for k in range(1, n_low)]

    class Gather:
        def __init__(self, buf, send, recv, count):
            self.buf, self.sent, self.got, self.count = buf, send, recv, count

        def copy(self, block, sem, where):
            ref = self.buf.at[block]
            return remote(ref, ref, self.sent.at[sem], self.got.at[block], expert=where)

        def start(self):
            for k in (*range(1, pairs, 2), *range(2, pairs, 2)):
                self.send(k)
            self.send(0)

        def send(self, k):
            zz = lax.rem(chip + k, pairs)

            @pl.when(me < self.count)
            def _():
                self.copy(me, zz, 2 * zz + core if k else sibling).start()

        def finish(self):
            for k in range(pairs - 1, 0, -1):
                zz = lax.rem(chip + k, pairs)
                src = 2 * zz + core

                @pl.when(src < self.count)
                def _():
                    self.copy(src, zz, src).wait_recv()
                    self.copy(src, pairs + zz, sibling).start()

            for k in range(pairs):
                zz = lax.rem(chip + k, pairs)
                src = 2 * zz + 1 - core

                @pl.when(src < self.count)
                def _():
                    self.copy(src, zz, sibling).wait_recv()

            @pl.when(me < self.count)
            def _():
                for k in range(1, pairs):
                    zz = lax.rem(chip + k, pairs)
                    self.copy(me, zz, 2 * zz + core).wait_send()
                self.copy(me, chip, sibling).wait_send()

            for k in range(1, pairs):
                zz = lax.rem(chip + k, pairs)
                src = 2 * zz + core

                @pl.when(src < self.count)
                def _():
                    self.copy(src, pairs + zz, sibling).wait_send()

    class Reduce:
        def __init__(self, count, rows, psend, precv, fsend, frecv, sems, result, halves=False):
            self.halves = halves
            self.count, self.rows, self.part = count, rows, pl.ds(0, rows)
            self.psend, self.precv, self.fsend, self.frecv = psend, precv, fsend, frecv
            self.sems, self.result = sems, result

        def pair_copy(self, zz):
            return remote(
                self.psend.at[zz, self.part],
                self.precv.at[zz, self.part],
                self.sems.at[0, zz],
                self.sems.at[1, zz],
                expert=sibling,
            )

        def far_copy(self, zz, slot, half=None):
            part = self.part if half is None else pl.ds(half * (self.rows // 2), self.rows // 2)
            at = 2 if half is None else 2 + 2 * half
            return remote(
                self.fsend.at[zz, part],
                self.frecv.at[slot, part],
                self.sems.at[at, zz],
                self.sems.at[at + 1, slot],
                expert=2 * zz + core,
            )

        def far_parts(self):
            return (0, 1) if self.halves else (None,)

        def far_copies(self, zz, slot):
            return [self.far_copy(zz, slot, half) for half in self.far_parts()]

        def start(self, make, send):
            for k in range(pairs):
                zz = lax.rem(chip + 1 + k, pairs)
                block = 2 * zz + 1 - core

                @pl.when(block < self.count)
                def _():
                    self.psend[zz, self.part] = make(block).astype(BF16)
                    self.pair_copy(zz).start()

            for k in range(1, pairs):
                zz = lax.rem(chip + k, pairs)
                block = 2 * zz + core

                @pl.when(block < self.count)
                def _():
                    mine = make(block)
                    self.pair_copy(zz).wait_recv()
                    self.fsend[zz, self.part] = (
                        mine + self.precv[zz, self.part].astype(F32)
                    ).astype(BF16)

                    def go():
                        for copy in self.far_copies(zz, chip):
                            copy.start()

                    if isinstance(send, bool):
                        if send:
                            go()
                    else:
                        pl.when(send)(go)

            @pl.when(me < self.count)
            def _():
                mine = make(me)
                self.pair_copy(chip).wait_recv()
                self.result[self.part] = mine + self.precv[chip, self.part].astype(F32)

            @pl.when(me >= self.count)
            def _():
                self.result[self.part] = jnp.zeros((self.rows, self.result.shape[1]), F32)

        def send(self, *parts):
            for k, half in parts:
                zz = lax.rem(chip + k, pairs)

                @pl.when(2 * zz + core < self.count)
                def _():
                    self.far_copy(zz, chip, self.far_parts()[half]).start()

        def finish(self):
            @pl.when(me < self.count)
            def _():
                for k in range(1, pairs):
                    zz = lax.rem(chip + k, pairs)
                    for copy in self.far_copies(zz, zz):
                        copy.wait_recv()
                    self.result[self.part] += self.frecv[zz, self.part].astype(F32)

            for k in range(pairs):
                zz = lax.rem(chip + 1 + k, pairs)

                @pl.when(2 * zz + 1 - core < self.count)
                def _():
                    self.pair_copy(zz).wait_send()

            for k in range(1, pairs):
                zz = lax.rem(chip + k, pairs)

                @pl.when(2 * zz + core < self.count)
                def _():
                    for copy in self.far_copies(zz, chip):
                        copy.wait_send()

    def attn_weight_copy(peer, slot):
        ref = w_all.at[me, shard_rows(slot)]
        return remote(ref, ref, w_send.at[peer], w_recv.at[slot], dp=peer)

    def up_low(peer, block):
        ref = up_w.at[shard_rows(high * n_low + block)]
        return remote(
            ref,
            ref,
            uw_send.at[peer],
            uw_recv.at[high * n_low + block],
            dp=high * n_low + peer,
        )

    def up_high(peer, row, block):
        ref = up_w.at[shard_rows(row * n_low + block)]
        return remote(
            ref,
            ref,
            uw_send_two.at[peer, block],
            uw_recv.at[row * n_low + block],
            dp=peer * n_low + low,
        )

    def down_high(peer, block):
        ref = down_w.at[shard_rows(block * n_low + low)]
        return remote(
            ref,
            ref,
            dw_send.at[peer],
            dw_recv.at[block * n_low + low],
            dp=peer * n_low + low,
        )

    def down_low(peer, column_at, block):
        ref = down_w.at[shard_rows(block * n_low + column_at)]
        return remote(
            ref,
            ref,
            dw_send_two.at[peer, block],
            dw_recv.at[block * n_low + column_at],
            dp=high * n_low + peer,
        )

    up_in = pltpu.make_async_copy(uw_hbm, ugrad_ref, in_sems.at[0])
    down_in = pltpu.make_async_copy(dw_hbm, dgrad_ref, in_sems.at[1])
    up_in.start()
    down_in.start()
    kv_k[...] = jnp.zeros_like(kv_k)
    barrier = pltpu.get_barrier_semaphore()
    for k in range(1, n_exp):
        pl.semaphore_signal(
            barrier, inc=1, device_id={"expert": lax.rem(me + k, n_exp)}, device_id_type=MESH
        )
    for k in range(1, n_dp):
        pl.semaphore_signal(
            barrier, inc=1, device_id={"dp": lax.rem(dp + k, n_dp)}, device_id_type=MESH
        )
    rows_all[1, me] = cot_ref[...]
    wrow[...] = jnp.zeros_like(wrow)
    w_all[me, shard_rows(dp)] = aw_ref[...].astype(BF16)
    up_in.wait()
    up_w[shard_rows(dp)] = ugrad_ref[...].astype(BF16)
    down_in.wait()
    down_w[shard_rows(dp)] = dgrad_ref[...].astype(BF16)
    pl.semaphore_wait(barrier, n_exp + n_dp - 2)
    each_peer(lambda peer: attn_weight_copy(peer, dp).start())
    cot_gather = Gather(rows_all.at[1], bg_send, bg_recv, n_act)
    cot_gather.send(2)
    for peer in low_peers():
        up_low(peer, low).start()
    for peer in high_peers():
        down_high(peer, high).start()
    for peer in high_peers():
        up_high(peer, high, low).start()
    for peer in low_peers():
        down_low(peer, low, high).start()

    kvb[...] = kvw_ref[...].astype(BF16)
    rb[...] = rw_ref[...].astype(BF16)
    gain_one = vec_ref[0:1, :]
    bias_one = vec_ref[1:2, :]
    gain_two = vec_ref[2:3, :]
    bias_two = vec_ref[3:4, :]
    halt = vec_ref[4:5, :]
    state[0] = x_ref[...].astype(F32)
    own_rows = pl.ds(pl.multiple_of(me * own, own), own)

    lane = lax.broadcasted_iota(jnp.int32, (own, LANES), 1)
    route_lane = lax.broadcasted_iota(jnp.int32, (own, 2 * n_exp), 1)
    lane_two = lax.broadcasted_iota(jnp.int32, (2 * own, LANES), 1)
    lane_cap = lax.broadcasted_iota(jnp.int32, (cap, LANES), 1)
    route_cap = lax.broadcasted_iota(jnp.int32, (cap, 2 * n_exp), 1)

    def column(values, index, lanes):
        return jnp.sum(jnp.where(lanes == index, values, 0.0), axis=1, keepdims=True)

    def cap_rows(loop):
        return pl.ds(pl.multiple_of(loop * cap, cap), cap)

    def window_keys(loop):
        return kv_k[loop, pl.ds(win_at, window)].reshape(keys, 2 * HD)

    def routing():
        position = lax.broadcasted_iota(jnp.int32, (1, slots), 1)
        bound = 0
        segment = jnp.zeros((1, slots), F32)
        for index in range(len_ref.shape[1]):
            bound = bound + len_ref[0, index]
            segment = segment + jnp.where(position >= bound, 1.0, 0.0)
        sub = lax.broadcasted_iota(jnp.int32, (n_exp, slots), 0)
        position_all = lax.broadcasted_iota(jnp.int32, (n_exp, slots), 1)
        valid = segment < len_ref.shape[1] - 0.5
        rowm_ref[LOOPS] = segment
        picks, selected = [], jnp.zeros((n_exp, slots), F32)
        for loop in range(LOOPS):
            running = jnp.where(valid & (run_ref[...] > loop), 1.0, 0.0)
            att = jnp.zeros((n_exp, slots), F32)
            for k in range(ar_ref.shape[1]):
                att = att + jnp.where(ar_ref[loop, k : k + 1, :] == sub, 1.0, 0.0)
            ffn = jnp.zeros((n_exp, slots), F32)
            mine = jnp.zeros((1, slots), F32)
            for k in range(fr_ref.shape[1]):
                ffn = ffn + jnp.where(fr_ref[loop, k : k + 1, :] == sub, 1.0, 0.0)
                mine = mine + jnp.where(fr_ref[loop, k : k + 1, :] == me, running, 0.0)
            picks.append((att, ffn, running))
            selected = selected + jnp.where(sub == loop, mine, 0.0)
        ranks = selected
        shift = 1
        while shift < slots:
            moved = pltpu.roll(ranks, shift, 1)
            ranks = ranks + jnp.where(position_all >= shift, moved, 0.0)
            shift *= 2
        ranks = jnp.where(selected > 0.5, ranks - 1.0, -1.0)
        for loop in range(LOOPS):
            att, ffn, running = picks[loop]
            rank = ranks[loop : loop + 1]
            rowm_ref[loop] = rank
            rest = jnp.where(
                sub == 0,
                rank,
                jnp.where(sub == 1, running, jnp.where(sub == 2, segment, 0.0)),
            )
            spare = jnp.zeros((INFO - 3 * n_exp, slots), F32)
            meta_ref[loop] = jnp.transpose(jnp.concatenate([att, ffn, rest, spare], axis=0))

    def kv_copy(loop, where, sem):
        ref = kv_k.at[loop, me]
        return remote(ref, ref, kg_send.at[sem], kg_recv.at[me], expert=where)

    def prepare(loop):
        unit, _ = normalise(state[loop])
        normed = (unit * gain_one + bias_one).astype(BF16)
        normed_k[loop] = normed
        kv_k[loop, me] = nn(normed, kvb[...]).astype(BF16)
        for k in range(1, window):

            @pl.when(me + k < n_act)
            def _():
                kv_copy(loop, me + k, k - 1).start()

        info = meta_ref[loop, own_rows, 0 : 2 * n_exp]
        gate_k[loop] = masked_softmax(
            nt(normed, rb[...]), (info > 0.5) & (route_lane < n_exp)
        )

    def running_rows(loop):
        return meta_ref[loop, own_rows, RUN_LANE : RUN_LANE + 1]

    each_peer(lambda peer: attn_weight_copy(peer, peer).wait_recv())
    weights_gather = Gather(w_all, wg_send, wg_recv, n_exp)
    weights_gather.start()
    routing()
    prepare(0)
    seg_own = meta_ref[0, own_rows, SEG_LANE : SEG_LANE + 1]
    key_cols = pl.ds(pl.multiple_of(win_at * own, own), keys)
    seg_keys = rowm_ref[LOOPS, :, key_cols]
    row_at = me * own + lax.broadcasted_iota(jnp.int32, (own, keys), 0)
    key_at = win_at * own + lax.broadcasted_iota(jnp.int32, (own, keys), 1)
    allowed = (seg_own == seg_keys) & (key_at <= row_at)
    bias[...] = jnp.where(allowed, 0.0, masked_score)
    up_acc[...] = jnp.zeros_like(up_acc)
    down_acc[...] = jnp.zeros_like(down_acc)
    attn_acc[...] = jnp.zeros_like(attn_acc)
    small_acc[...] = jnp.zeros_like(small_acc)
    weights_gather.finish()
    for block in low_peers():
        up_low(block, block).wait_recv()
        for peer in high_peers():
            up_high(peer, high, block).start()
    for block in high_peers():
        down_high(block, block).wait_recv()
        for peer in low_peers():
            down_low(peer, low, block).start()

    def attention(loop):
        normed = normed_k[loop]

        def queries(expert, none):
            query = jnp.where(lane < HD, nn(normed, w_all[expert]), 0.0).astype(BF16)
            q_k[loop, pl.ds(pl.multiple_of(expert * own, own), own)] = query
            return none

        lax.fori_loop(0, n_exp, queries, 0, unroll=True)
        running = running_rows(loop)
        gates = gate_k[loop] * running
        mix[...] = jnp.zeros_like(mix)
        for k in range(1, window):

            @pl.when(active & (me >= k))
            def _():
                ref = kv_k.at[loop, me - k]
                remote(
                    ref, ref, kg_send.at[k - 1], kg_recv.at[me - k], expert=me - k
                ).wait_recv()

        kv_rows = window_keys(loop)

        def attend(pair, none):
            rows = pl.ds(pl.multiple_of(pair * 2 * own, 2 * own), 2 * own)
            scores = nt(q_k[loop, rows], kv_rows) * scale
            scores = (scores.reshape(2, own, keys) + bias[...][None]).reshape(2 * own, keys)
            powers = jnp.exp(scores - jnp.max(scores, axis=1, keepdims=True))
            prob = (powers * (1.0 / jnp.sum(powers, axis=1, keepdims=True))).astype(BF16)
            p_k[loop, rows] = prob
            outs = jnp.where(lane_two < HD, 0.0, nn(prob, kv_rows)).astype(BF16)
            o_k[loop, rows] = outs
            for half in range(2):
                expert = 2 * pair + half
                gate = column(gates, expert, route_lane)
                mix[...] += gate * nt(outs[half * own : (half + 1) * own], w_all[expert])
            return none

        lax.fori_loop(0, n_exp // 2, attend, 0, unroll=True)
        for k in range(1, window):

            @pl.when(me + k < n_act)
            def _():
                kv_copy(loop, me + k, k - 1).wait_send()

        centre = state[loop] + mix[...]
        middle[loop] = centre
        unit, _ = normalise(centre)
        second = (unit * gain_two + bias_two).astype(BF16)
        second_k[loop] = second
        rows_all[0, me] = second

    rows_gather = Gather(rows_all.at[0], ag_send, ag_recv, n_act)
    factor_gather = Gather(wrow, fg_send, fg_recv, n_act)

    def place_matrices(loop):
        ranks = rowm_ref[loop, :, 0:valid_rows]
        slot = lax.broadcasted_iota(jnp.int32, (cap, valid_rows), 0).astype(F32)
        gather_m[...] = jnp.where(slot == ranks, 1.0, 0.0).astype(BF16)
        slot = lax.broadcasted_iota(jnp.int32, (own, cap), 1).astype(F32)

        def block_matrix(block, none):
            rows = pl.ds(pl.multiple_of(block * own, own), own)
            ranks = meta_ref[loop, rows, RANK_LANE : RANK_LANE + 1]
            scatter_m[rows] = jnp.where(slot == ranks, 1.0, 0.0).astype(BF16)
            return none

        lax.fori_loop(0, n_act, block_matrix, 0)

    def scatter_rows(block):
        return scatter_m[pl.ds(pl.multiple_of(block * own, own), own)]

    def take(buf):
        return nn(gather_m[...], rows_all[buf, 0:n_act].reshape(valid_rows, width))

    def expert_rows(loop):
        rows_in = take(0).astype(BF16)
        rows_k[cap_rows(loop)] = rows_in
        allowed_lanes = (chosen_k[...] > 0.5) & (route_cap >= n_exp)
        gate = column(masked_softmax(nt(rows_in, rb[...]), allowed_lanes), n_exp + me, route_cap)
        fgate_k[cap_rows(loop)] = gate
        part_k[cap_rows(loop)] = jnp.zeros((cap, width), F32)

    root = math.sqrt(2.0 / math.pi)

    def tile_cols(tile):
        return pl.ds(pl.multiple_of(tile * TILE, TILE), TILE)

    def hidden_layer(loop):
        rows_in = rows_k[cap_rows(loop)]

        def step(tile, none):
            cols = tile_cols(tile)
            inner = nn(rows_in, up_w[:, cols])
            square = inner * inner
            curve = jnp.tanh(root * inner * (1.0 + 0.044715 * square))
            upper = 0.5 * (1.0 + curve)
            hidden = (inner * upper).astype(BF16)
            hid[cap_rows(loop), cols] = hidden
            slope = upper + 0.5 * inner * (1.0 - curve * curve) * (
                root + (3.0 * 0.044715 * root) * square
            )
            gprime[cap_rows(loop), cols] = slope.astype(BF16)
            part_k[cap_rows(loop)] += nt(hidden, down_w[:, cols])
            return none

        lax.fori_loop(0, tiles, step, 0, unroll=True)

    sums = Reduce(
        n_act,
        own,
        pair_send_two,
        pair_recv_two,
        far_send_two,
        far_recv_two,
        rs_sems_two,
        total_two,
        True,
    )
    back_sums = Reduce(
        n_act, own + EXTRA, pair_send, pair_recv, far_send, far_recv, rs_sems, total
    )

    def start_terms(loop, send):
        terms = (part_k[cap_rows(loop)] * fgate_k[cap_rows(loop)]).astype(BF16)
        sums.start(lambda block: nn(scatter_rows(block), terms), send)

    def wait_weights():
        for peer in high_peers():
            for block in range(n_low):
                up_high(peer, peer, block).wait_recv()
        for peer in low_peers():
            for block in range(n_high):
                down_low(peer, peer, block).wait_recv()

    def chances():
        chance_one = jax.nn.sigmoid(jnp.sum(state[1] * halt, axis=1, keepdims=True))
        chance_two = jax.nn.sigmoid(jnp.sum(state[2] * halt, axis=1, keepdims=True))
        return chance_one, chance_two

    def last_factor():
        chance_one, chance_two = chances()
        weight_last = (1.0 - chance_one) * (1.0 - chance_two)
        sgrad[last] = weight_last * cot_ref[...].astype(F32)
        upper = weight_last.astype(BF16).astype(F32)
        factors = jnp.where(lane == 0, upper, jnp.where(lane == 1, weight_last - upper, 0.0))
        wrow[me] = jnp.transpose(factors)[0:EXTRA].astype(BF16)
        factor_gather.start()

    carry[...] = jnp.zeros_like(carry)

    def state_grads(loop_dot):
        chance_one, chance_two = chances()
        cot = cot_ref[...].astype(F32)
        first, next_one = state[1], state[2]
        stay = 1.0 - chance_one
        weight_two = stay * chance_two
        weight_three = stay * (1.0 - chance_two)
        dot_one = jnp.sum(cot * first, axis=1, keepdims=True)
        dot_two = jnp.sum(cot * next_one, axis=1, keepdims=True)
        dot_middle = jnp.sum(cot * middle[last], axis=1, keepdims=True)
        dot_three = jnp.where(
            running_rows(last) > 0.5, weight_three * dot_middle + loop_dot, weight_three * dot_two
        )
        slope_one = chance_one * (stay * dot_one - weight_two * dot_two - dot_three)
        slope_two = chance_two * (weight_three * dot_two - dot_three)
        sgrad[0] = chance_one * cot + slope_one * halt
        sgrad[1] = weight_two * cot + slope_two * halt
        small_acc[vec_at + 4 : vec_at + 5] = jnp.sum(
            slope_one * first + slope_two * next_one, axis=0, keepdims=True
        )

    def finish_output():
        chance_one, chance_two = chances()
        first, next_one = state[1], state[2]
        final = jnp.where(running_rows(last) > 0.5, middle[last] + total_two[0:own], next_one)
        stay = 1.0 - chance_one
        out_ref[...] = (
            chance_one * first + stay * chance_two * next_one + stay * (1.0 - chance_two) * final
        )

    vec_at = 2 * HD + EXTRA

    def expert_back(loop):
        grad_rows = row_grads[...]
        gate = fgate_k[cap_rows(loop)]
        ggrad[...] = jnp.sum(grad_rows * part_k[cap_rows(loop)], axis=1, keepdims=True)
        scaled = (grad_rows * gate).astype(BF16)
        scaled_k[...] = scaled
        row_grads[...] = jnp.zeros_like(row_grads)

        def step(tile, none):
            cols = tile_cols(tile)
            inner_grad = (
                nn(scaled, down_w[:, cols]) * gprime[cap_rows(loop), cols].astype(F32)
            ).astype(BF16)
            gprime[cap_rows(loop), cols] = inner_grad
            row_grads[...] += nt(inner_grad, up_w[:, cols])
            return none

        lax.fori_loop(0, tiles, step, 0, unroll=True)
        terms = row_grads[...].astype(BF16)
        gate_grad = ggrad[...]
        upper = gate_grad.astype(BF16).astype(F32)
        spread = jnp.where(lane_cap == n_exp + me, upper, 0.0) + jnp.where(
            lane_cap == me, gate_grad - upper, 0.0
        )
        spread_t = jnp.transpose(spread)[0:EXTRA].astype(BF16)

        def row_terms(block):
            matrix = scatter_rows(block)
            grads = nt(spread_t, matrix)
            return jnp.concatenate(
                [
                    nn(matrix, terms),
                    jnp.concatenate([grads, jnp.zeros((EXTRA, width - own), F32)], axis=1),
                ],
                axis=0,
            )

        back_sums.start(row_terms, True)

    def expert_weights(loop):
        rows_in = rows_k[cap_rows(loop)]
        scaled = scaled_k[...]

        def step(tile, none):
            cols = tile_cols(tile)
            down_acc[:, cols] += tn(scaled, hid[cap_rows(loop), cols])
            up_acc[:, cols] += tn(rows_in, gprime[cap_rows(loop), cols])
            return none

        lax.fori_loop(0, tiles, step, 0, unroll=True)

    def order_at(source, receiver, count):
        return lax.rem(source - receiver + count, count) - 1

    spare = width // shard

    def up_grad_first(peer, slot, block, receiver):
        return remote(
            hid.at[shard_rows(block * n_low + peer)],
            u_first.at[order_at(slot, receiver, n_low), shard_rows(block)],
            ug_send.at[peer, block],
            ug_recv.at[slot, block],
            dp=high * n_low + peer,
        )

    def up_grad_second(peer, slot, receiver):
        return remote(
            hid.at[shard_rows(spare + peer)],
            u_last.at[order_at(slot, receiver, n_high)],
            ug_send_two.at[peer],
            ug_recv_two.at[slot],
            dp=peer * n_low + low,
        )

    def down_grad_first(peer, slot, block, receiver):
        return remote(
            gprime.at[shard_rows(peer * n_low + block)],
            d_first.at[order_at(slot, receiver, n_high), shard_rows(block)],
            dg_send.at[peer, block],
            dg_recv.at[slot, block],
            dp=peer * n_low + low,
        )

    def down_grad_second(peer, slot, receiver):
        return remote(
            gprime.at[shard_rows(spare + peer)],
            d_last.at[order_at(slot, receiver, n_low)],
            dg_send_two.at[peer],
            dg_recv_two.at[slot],
            dp=high * n_low + peer,
        )

    def send_expert_weights():
        hid[0:width] = up_acc[...].astype(BF16)
        for peer in low_peers():
            for block in high_peers():
                up_grad_first(peer, low, block, peer).start()
        gprime[0:width] = down_acc[...].astype(BF16)
        for peer in high_peers():
            for block in low_peers():
                down_grad_first(peer, high, block, peer).start()
        for peer in low_peers():
            up_grad_first(peer, low, high, peer).start()
        for peer in high_peers():
            down_grad_first(peer, high, low, peer).start()

    def pass_expert_weights():
        for block in high_peers():
            added = up_acc[shard_rows(block * n_low + low)]
            for peer in low_peers():
                up_grad_first(peer, peer, block, low).wait_recv()
                added = added + u_first[
                    order_at(peer, low, n_low), shard_rows(block)
                ].astype(F32)
            hid[shard_rows(spare + block)] = added.astype(BF16)
            up_grad_second(block, high, block).start()
        for block in low_peers():
            added = down_acc[shard_rows(high * n_low + block)]
            for peer in high_peers():
                down_grad_first(peer, peer, block, high).wait_recv()
                added = added + d_first[
                    order_at(peer, high, n_high), shard_rows(block)
                ].astype(F32)
            gprime[shard_rows(spare + block)] = added.astype(BF16)
            down_grad_second(block, low, block).start()

    def finish_expert_weights():
        added = up_acc[shard_rows(dp)]
        for peer in low_peers():
            up_grad_first(peer, peer, high, low).wait_recv()
            added = added + u_first[order_at(peer, low, n_low), shard_rows(high)].astype(F32)
        for peer in high_peers():
            up_grad_second(peer, peer, high).wait_recv()
            added = added + u_last[order_at(peer, high, n_high)].astype(F32)
        ugrad_ref[...] = added
        added = down_acc[shard_rows(dp)]
        for peer in high_peers():
            down_grad_first(peer, peer, low, high).wait_recv()
            added = added + d_first[order_at(peer, high, n_high), shard_rows(low)].astype(F32)
        for peer in low_peers():
            down_grad_second(peer, peer, low).wait_recv()
            added = added + d_last[order_at(peer, low, n_low)].astype(F32)
        dgrad_ref[...] = added

    attn_sums = Reduce(
        n_exp,
        2 * HD,
        pair_send_two,
        pair_recv_two,
        far_send_two,
        far_recv_two,
        a_sems,
        total_two,
    )

    def dkv_copy(distance, owner):
        return remote(
            dkv_send.at[jnp.clip(owner - win_at, 0, window - 1)],
            dkv_recv.at[distance - 1],
            dk_send.at[distance - 1],
            dk_recv.at[distance - 1],
            expert=owner,
        )

    def attention_back(loop, step):
        info = meta_ref[loop, own_rows, 0 : 2 * n_exp]
        running = running_rows(loop)
        branch = (sgrad[loop] + carry[...]) * running
        second_grad = total[0:own]
        gate_rows = total[own : own + n_exp, 0:own] + total[own + n_exp : own + 2 * n_exp, 0:own]
        gate_rows = jnp.concatenate(
            [jnp.zeros((n_exp, own), F32), gate_rows, jnp.zeros((LANES - 2 * n_exp, own), F32)],
            axis=0,
        )
        gate_grads = jnp.transpose(gate_rows)[:, 0 : 2 * n_exp]
        second = second_k[loop]
        gates = masked_softmax(nt(second, rb[...]), (info > 0.5) & (route_lane >= n_exp))
        loop_dot = jnp.sum(gates * gate_grads, axis=1, keepdims=True)
        logit_grad = (gates * (gate_grads - loop_dot)).astype(BF16)
        second_grad = second_grad + nn(logit_grad, rb[...])
        unit, inverse = normalise(middle[loop])
        middle_grad = norm_back(second_grad, unit, inverse, gain_two) + branch
        mgrad[...] = middle_grad

        gates = gate_k[loop]
        kv_rows = window_keys(loop)
        dkv_t[...] = jnp.zeros_like(dkv_t)

        def scores_back(pair, none):
            rows = pl.ds(pl.multiple_of(pair * 2 * own, 2 * own), 2 * own)
            out_grads = []
            for half in range(2):
                expert = 2 * pair + half
                part_grad = (column(gates, expert, route_lane) * mgrad[...]).astype(BF16)
                out_grads.append(
                    jnp.where(lane < HD, 0.0, nn(part_grad, w_all[expert])).astype(BF16)
                )
            out_grad = jnp.concatenate(out_grads, axis=0)
            prob_low = p_k[loop, rows]
            prob = prob_low.astype(F32)
            prob_grad = nt(out_grad, kv_rows)
            centre = jnp.sum(prob * prob_grad, axis=1, keepdims=True)
            score_grad = (prob * (prob_grad - centre)).astype(BF16)
            ds_k[rows] = score_grad
            dkv_t[...] += tn(q_k[loop, rows], score_grad) * scale + tn(out_grad, prob_low)
            return none

        lax.fori_loop(0, n_exp // 2, scores_back, 0, unroll=True)
        for block in range(window):
            grads = jnp.transpose(dkv_t[:, block * own : (block + 1) * own])
            dkv[block] = grads
            dkv_send[block] = grads.astype(BF16)
        for distance in range(1, window):

            @pl.when(active & (me >= distance))
            def _():
                dkv_copy(distance, me - distance).start()

        @pl.when(step == last)
        def _():
            state_grads(loop_dot)
            sums.send((1, 0))

        @pl.when(step == last + 1)
        def _():
            sums.send((3, 1))

        small_acc[2 * HD : vec_at] += tn(logit_grad, second)
        small_acc[vec_at + 2 : vec_at + 3] += jnp.sum(second_grad * unit, axis=0, keepdims=True)
        small_acc[vec_at + 3 : vec_at + 4] += jnp.sum(second_grad, axis=0, keepdims=True)
        normed = normed_k[loop]
        mix[...] = jnp.zeros_like(mix)
        dga[...] = jnp.zeros_like(dga)

        def queries_back(pair, none):
            rows = pl.ds(pl.multiple_of(pair * 2 * own, 2 * own), 2 * own)
            outs = o_k[loop, rows]
            query_grad = jnp.where(lane_two < HD, nn(ds_k[rows], kv_rows) * scale, 0.0).astype(BF16)
            for half in range(2):
                expert = 2 * pair + half
                cut = slice(half * own, (half + 1) * own)
                middle_grad = mgrad[...]
                dot = jnp.sum(middle_grad * nt(outs[cut], w_all[expert]), axis=1, keepdims=True)
                dga[...] += jnp.where(route_lane == expert, dot, 0.0)
                part_grad = (column(gates, expert, route_lane) * middle_grad).astype(BF16)
                attn_acc[expert] += tn(query_grad[cut], normed) + tn(outs[cut], part_grad)
                mix[...] += nt(query_grad[cut], w_all[expert])
            return none

        lax.fori_loop(0, n_exp // 2, queries_back, 0)

        @pl.when(loop == 0)
        def _():
            attn_sums.start(lambda block: attn_acc[block], False)

        gate_grads = dga[...]
        logit_grad = (
            gates * (gate_grads - jnp.sum(gates * gate_grads, axis=1, keepdims=True))
        ).astype(BF16)
        small_acc[2 * HD : vec_at] += tn(logit_grad, normed)
        normed_grad = mix[...] + nn(logit_grad, rb[...])
        unit, inverse = normalise(state[loop])

        own_block = jnp.clip(me - win_at, 0, window - 1)
        dkv[window] = jnp.where(active, dkv[own_block], 0.0)
        for distance in range(1, window):

            @pl.when(me + distance < n_act)
            def _():
                remote(
                    dkv_send.at[0],
                    dkv_recv.at[distance - 1],
                    dk_send.at[distance - 1],
                    dk_recv.at[distance - 1],
                    expert=me + distance,
                ).wait_recv()
                dkv[window] += dkv_recv[distance - 1].astype(F32)

        for distance in range(1, window):

            @pl.when(active & (me >= distance))
            def _():
                dkv_copy(distance, me - distance).wait_send()

        kv_grad = dkv[window].astype(BF16)
        small_acc[0 : 2 * HD] += tn(kv_grad, normed)
        normed_grad = normed_grad + nt(kv_grad, kvb[...])
        small_acc[vec_at : vec_at + 1] += jnp.sum(normed_grad * unit, axis=0, keepdims=True)
        small_acc[vec_at + 1 : vec_at + 2] += jnp.sum(normed_grad, axis=0, keepdims=True)
        carry[...] = (
            (sgrad[loop] + carry[...]) * (1.0 - running)
            + mgrad[...]
            + norm_back(normed_grad, unit, inverse, gain_one)
        )

    def phase(step, none):
        loop = jnp.where(step <= last, step, 2 * last - step)

        @pl.when(step <= last)
        def _():
            attention(loop)

        @pl.when(step == 2 * last)
        def _():
            sums.finish()
            finish_output()

        @pl.when(step > last)
        def _():
            rows_all[0, me] = ((sgrad[loop] + carry[...]) * running_rows(loop)).astype(BF16)

        rows_gather.start()
        place_matrices(loop)

        @pl.when(step <= last)
        def _():
            chosen_k[...] = nn(
                gather_m[...], meta_ref[loop, 0:valid_rows, 0 : 2 * n_exp].astype(BF16)
            )

        @pl.when(step == 0)
        def _():
            wait_weights()

        @pl.when(step == last)
        def _():
            cot_gather.finish()
            factor_gather.finish()

        rows_gather.finish()

        @pl.when(step == 0)
        def _():
            cot_gather.send(0)
            cot_gather.send(1)

        @pl.when(step == 1)
        def _():
            cot_gather.send(3)

        @pl.when(step <= last)
        def _():
            expert_rows(loop)
            hidden_layer(loop)

        @pl.when(step == last + 1)
        def _():
            sums.send((2, 1))

        @pl.when(step >= last)
        def _():
            factors = nt(
                gather_m[...], jnp.concatenate([wrow[block] for block in range(n_act)], axis=1)
            )
            factor = jnp.where(step == last, factors[:, 0:1] + factors[:, 1:2], 1.0)
            row_grads[...] = take(jnp.where(step == last, 1, 0)) * factor
            expert_back(loop)

        @pl.when(step <= last)
        def _():
            start_terms(loop, step < last)

        @pl.when(step < last)
        def _():
            sums.finish()
            state[loop + 1] = jnp.where(
                running_rows(loop) > 0.5, middle[loop] + total_two[0:own], state[loop]
            )
            prepare(loop + 1)

        @pl.when(step == last - 1)
        def _():
            last_factor()

        @pl.when(step >= last)
        def _():
            expert_weights(loop)

            @pl.when(step == 2 * last)
            def _():
                send_expert_weights()

            back_sums.finish()

            @pl.when(step == last)
            def _():
                sums.send((2, 0))

            @pl.when(step == last + 1)
            def _():
                sums.send((3, 0), (1, 1))

            attention_back(loop, step)

        return none

    lax.fori_loop(0, 2 * last + 1, phase, 0)
    xgrad_ref[...] = carry[...]

    chunk = small_acc.shape[0] // n_exp
    small_sums = Reduce(
        n_exp, chunk, s_pair_send, s_pair_recv, s_far_send, s_far_recv, s_sems, s_total
    )
    small_sums.start(
        lambda block: small_acc[pl.ds(pl.multiple_of(block * chunk, chunk), chunk)], True
    )
    attn_sums.send((1, 0), (3, 0), (2, 0))

    def attn_copy(peer, slot):
        return remote(
            a_stage.at[shard_rows(peer)],
            a_recv.at[shard_rows(slot)],
            t_send.at[1, peer],
            t_recv.at[1, slot],
            dp=peer,
        )

    def small_copy(peer, slot):
        return remote(
            s_dp.at[slot], s_dp.at[slot], t_send.at[0, peer], t_recv.at[0, slot], dp=peer
        )

    small_sums.finish()
    s_dp[dp] = s_total[...].astype(BF16)
    each_peer(lambda peer: small_copy(peer, dp).start())
    pass_expert_weights()
    attn_sums.finish()
    a_total[...] = jnp.transpose(total_two[...])
    a_stage[...] = a_total[...].astype(BF16)
    each_peer(lambda peer: attn_copy(peer, dp).start())
    each_peer(lambda peer: small_copy(peer, peer).wait_recv())
    s_total[...] = jnp.zeros_like(s_total)

    def add_small(index, none):
        s_total[...] += s_dp[index].astype(F32)
        return none

    lax.fori_loop(0, n_dp, add_small, 0)
    s_all[me] = s_total[...]
    small_gather = Gather(s_all, sg_send, sg_recv, n_exp)
    small_gather.start()
    agrad_ref[...] = a_total[shard_rows(dp)]

    def add_attn(peer):
        attn_copy(peer, peer).wait_recv()
        agrad_ref[...] += a_recv[shard_rows(peer)].astype(F32)

    each_peer(add_attn)
    finish_expert_weights()
    small_gather.finish()
    small = s_all[...].reshape(n_exp * chunk, width)
    kvgrad_ref[...] = jnp.transpose(small[0 : 2 * HD])
    rgrad_ref[...] = small[2 * HD : vec_at]
    vgrad_ref[...] = small[vec_at : vec_at + 8]

    def sent(peer):
        attn_weight_copy(peer, dp).wait_send()
        small_copy(peer, dp).wait_send()
        attn_copy(peer, dp).wait_send()

    each_peer(sent)
    for peer in low_peers():
        up_low(peer, low).wait_send()
        down_grad_second(peer, low, peer).wait_send()
        for block in range(n_high):
            down_low(peer, low, block).wait_send()
            up_grad_first(peer, low, block, peer).wait_send()
    for peer in high_peers():
        down_high(peer, high).wait_send()
        for block in range(n_low):
            up_high(peer, high, block).wait_send()
            down_grad_first(peer, high, block, peer).wait_send()
        up_grad_second(peer, high, peer).wait_send()


def adam_kernel(*refs):
    out_in, xgrad_in, ugrad, dgrad, agrad, kvgrad, rgrad, vgrad = refs[:8]
    shared, kv, router, attn, up, down = (refs[8 + 3 * index : 11 + 3 * index] for index in range(6))
    out, xgrad = refs[26:28]
    shared_out, kv_out, router_out, attn_out, up_out, down_out = (
        refs[28:31],
        refs[31:34],
        refs[34:37],
        refs[37:41],
        refs[41:45],
        refs[45:49],
    )

    def update(sources, grad, results, rate, decay):
        values = adam_update(*(source[...] for source in sources), grad, rate, decay)
        for result, value in zip(results, values):
            result[...] = value
        if len(results) > 3:
            results[3][...] = values[0].astype(BF16)

    out[...] = out_in[...]
    xgrad[...] = xgrad_in[...]
    update(up, ugrad[...], up_out, 14.0 / math.sqrt(D), decay_rate)
    update(down, dgrad[...], down_out, 17.0 / math.sqrt(FF), decay_rate)

    @pl.when(pl.program_id(0) == 0)
    def _():
        row = lax.broadcasted_iota(jnp.int32, shared[0].shape, 0)
        rates = jnp.where(row < 4, 6.0, 20.0 / math.sqrt(D))
        update(shared, vgrad[0 : shared[0].shape[0]], shared_out, rates, 0.0)
        update(kv, kvgrad[...], kv_out, 20.0 / math.sqrt(D), decay_rate)
        update(router, rgrad[...], router_out, 50.0 / math.sqrt(3 * D), decay_rate)
        lane = lax.broadcasted_iota(jnp.int32, attn[0].shape, 1)
        rates = jnp.where(lane < HD, 25.0 / math.sqrt(D), 50.0 / math.sqrt(HD))
        update(attn, agrad[...], attn_out, rates, decay_rate)


def dp_grid(n_dp):
    n_low = 1
    while n_low * n_low * 4 <= n_dp:
        n_low *= 2
    return n_low, n_dp // n_low


def per_device(
    block_input,
    cotangent,
    lengths,
    run_loops,
    attn_routes,
    ffn_routes,
    shared_vectors,
    shared_moment,
    shared_second,
    key_value,
    kv_moment,
    kv_second,
    router_weights,
    router_moment,
    router_second,
    attn_weights,
    attn_moment,
    attn_second,
    up_weights,
    up_moment,
    up_second,
    down_weights,
    down_moment,
    down_second,
):
    n_exp = lax.axis_size("expert")
    n_dp = lax.axis_size("dp")
    own, width = block_input.shape
    slots = run_loops.shape[0]
    shard = attn_weights.shape[1]
    hidden = up_weights.shape[2]
    cap = 5 * slots * KFF // (4 * n_exp)
    n_act = FILLED // own
    window = min(n_act, MAXLEN // own + 1)
    pairs = n_exp // 2
    valid_rows = n_act * own
    n_low, n_high = dp_grid(n_dp)

    small_rows = 32 * n_exp
    vmem = pltpu.VMEM
    dma = pltpu.SemaphoreType.DMA
    block = (pairs, own + EXTRA, width)
    small_block = (pairs, 32, width)
    scratch = [
        vmem((LOOPS, slots, INFO), F32),
        vmem((LOOPS + 1, 1, slots), F32),
        vmem((width, 2 * HD), BF16),
        vmem((2 * n_exp, width), BF16),
        vmem((n_exp, width, 2 * HD), BF16),
        vmem((width, hidden), BF16),
        vmem((width, hidden), BF16),
        vmem((width, hidden), F32),
        vmem((width, hidden), F32),
        vmem((n_exp, 2 * HD, width), F32),
        vmem((small_rows, width), F32),
        vmem((LOOPS, own, width), F32),
        vmem((LOOPS, own, width), F32),
        vmem((LOOPS, own, width), BF16),
        vmem((LOOPS, own, width), BF16),
        vmem((LOOPS, n_exp, own, 2 * HD), BF16),
        vmem((LOOPS, n_exp * own, 2 * HD), BF16),
        vmem((LOOPS, n_exp * own, 2 * HD), BF16),
        vmem((LOOPS, n_exp * own, window * own), BF16),
        vmem((n_exp * own, window * own), BF16),
        vmem((own, window * own), F32),
        vmem((own, width), F32),
        vmem((own, 2 * n_exp), F32),
        vmem((2 * HD, window * own), F32),
        vmem((window + 1, own, 2 * HD), F32),
        vmem((LOOPS, own, 2 * n_exp), F32),
        vmem((2, n_exp, own, width), BF16),
        vmem((n_exp, EXTRA, own), BF16),
        vmem((cap, valid_rows), BF16),
        vmem((valid_rows, cap), BF16),
        vmem((LOOPS * cap, width), BF16),
        vmem((LOOPS * cap, hidden), BF16),
        vmem((LOOPS * cap, hidden), BF16),
        vmem((cap, width), F32),
        vmem((LOOPS * cap, width), F32),
        vmem((LOOPS * cap, 1), F32),
        vmem((cap, 2 * n_exp), F32),
        vmem((cap, 1), F32),
        vmem((cap, width), BF16),
        vmem((LOOPS, own, width), F32),
        vmem((own, width), F32),
        vmem((own, width), F32),
        vmem((own + EXTRA, width), F32),
        vmem((own, width), F32),
        vmem(block, BF16),
        vmem(block, BF16),
        vmem(block, BF16),
        vmem(block, BF16),
        vmem((pairs, own, width), BF16),
        vmem((pairs, own, width), BF16),
        vmem((pairs, own, width), BF16),
        vmem((pairs, own, width), BF16),
        vmem((window, own, 2 * HD), BF16),
        vmem((window, own, 2 * HD), BF16),
        vmem((n_low - 1, n_high * shard, hidden), BF16),
        vmem((n_high - 1, shard, hidden), BF16),
        vmem((n_high - 1, n_low * shard, hidden), BF16),
        vmem((n_low - 1, shard, hidden), BF16),
        vmem((width, 2 * HD), F32),
        vmem((width, 2 * HD), BF16),
        vmem((width, 2 * HD), BF16),
        vmem(small_block, BF16),
        vmem(small_block, BF16),
        vmem(small_block, BF16),
        vmem(small_block, BF16),
        vmem((32, width), F32),
        vmem((n_dp, 32, width), BF16),
        vmem((n_exp, 32, width), F32),
        dma((2,)),
        dma((n_dp,)),
        dma((n_dp,)),
        dma((n_low,)),
        dma((n_dp,)),
        dma((n_high, n_low)),
        dma((n_high,)),
        dma((n_dp,)),
        dma((n_low, n_high)),
        dma((2 * pairs,)),
        dma((n_exp,)),
        dma((2 * pairs,)),
        dma((n_exp,)),
        dma((2 * pairs,)),
        dma((n_exp,)),
        dma((2 * pairs,)),
        dma((n_exp,)),
        dma((2 * pairs,)),
        dma((n_exp,)),
        dma((window,)),
        dma((n_exp,)),
        dma((4, pairs)),
        dma((6, pairs)),
        dma((4, pairs)),
        dma((4, pairs)),
        dma((window,)),
        dma((window,)),
        dma((n_low, n_high)),
        dma((n_low, n_high)),
        dma((n_high,)),
        dma((n_high,)),
        dma((n_high, n_low)),
        dma((n_high, n_low)),
        dma((n_low,)),
        dma((n_low,)),
        dma((2, n_dp)),
        dma((2, n_dp)),
    ]
    whole = pl.BlockSpec(memory_space=pltpu.VMEM)
    scalars = pl.BlockSpec(memory_space=pltpu.SMEM)
    outside = pl.BlockSpec(memory_space=pl.ANY)
    shape = jax.ShapeDtypeStruct
    sums = pl.pallas_call(
        functools.partial(block_kernel, n_exp, n_dp, n_act, cap),
        out_shape=(
            shape((own, width), F32),
            shape((own, width), F32),
            shape((shard, hidden), F32),
            shape((shard, hidden), F32),
            shape((shard, 2 * HD), F32),
            shape((width, 2 * HD), F32),
            shape((2 * n_exp, width), F32),
            shape((8, width), F32),
        ),
        in_specs=[whole, whole, scalars, *([whole] * 7), outside, outside],
        out_specs=[whole] * 8,
        scratch_shapes=scratch,
        compiler_params=pltpu.CompilerParams(
            collective_id=0, has_side_effects=True, vmem_limit_bytes=63 * 1024 * 1024
        ),
        name="block",
    )(
        block_input,
        cotangent,
        lengths,
        run_loops[None],
        attn_routes.transpose(0, 2, 1),
        ffn_routes.transpose(0, 2, 1),
        shared_vectors,
        key_value,
        router_weights.T,
        attn_weights[0],
        up_weights[0],
        down_weights[0],
    )

    steps = max(1, shard // 64)
    rows = shard // steps

    def by_rows(array):
        return pl.BlockSpec((array.shape[0] // steps, array.shape[1]), lambda step: (step, 0))

    def fixed(array):
        return pl.BlockSpec(array.shape, lambda step: (0, 0))

    output, input_grad, up_sum, down_sum, *small = sums
    small_args = [
        shared_vectors,
        shared_moment,
        shared_second,
        key_value,
        kv_moment,
        kv_second,
        router_weights.T,
        router_moment.T,
        router_second.T,
        attn_weights[0],
        attn_moment[0],
        attn_second[0],
    ]
    large_args = [
        up_weights[0],
        up_moment[0],
        up_second[0],
        down_weights[0],
        down_moment[0],
        down_second[0],
    ]
    attn_low = shape((shard, 2 * HD), BF16)
    large_low = shape((shard, hidden), BF16)
    like = [shape(array.shape, array.dtype) for array in small_args]
    big = [shape(array.shape, array.dtype) for array in large_args]
    outs = [
        shape(output.shape, F32),
        shape(input_grad.shape, F32),
        *like,
        attn_low,
        *big[:3],
        large_low,
        *big[3:],
        large_low,
    ]
    results = pl.pallas_call(
        adam_kernel,
        grid=(steps,),
        out_shape=outs,
        in_specs=[
            by_rows(output),
            by_rows(input_grad),
            by_rows(up_sum),
            by_rows(down_sum),
            *(fixed(array) for array in small),
            *(fixed(array) for array in small_args),
            *(by_rows(array) for array in large_args),
        ],
        out_specs=[
            by_rows(output),
            by_rows(input_grad),
            *(fixed(array) for array in (*like, attn_low)),
            *(by_rows(array) for array in (*big[:3], large_low, *big[3:], large_low)),
        ],
        compiler_params=pltpu.CompilerParams(vmem_limit_bytes=63 * 1024 * 1024),
        name="adamw",
    )(*sums, *small_args, *large_args)
    output, input_grad, *rest = results
    shared_kv, router, weights = rest[:6], rest[6:9], rest[9:]
    return (
        output,
        input_grad,
        *shared_kv,
        *(array.T for array in router),
        *(array[None] for array in weights),
    )


def solution(mesh):
    rows = P(("dp", "expert"), None)
    weights = P("expert", "dp", None)
    return jax.shard_map(
        per_device,
        mesh=mesh,
        in_specs=(
            rows,
            rows,
            P("dp", None),
            P("dp"),
            P(None, "dp", None),
            P(None, "dp", None),
            *([P()] * 9),
            *([weights] * 9),
        ),
        out_specs=(rows, rows, *([P()] * 9), *([weights] * 12)),
        check_vma=False,
    )
```

profile of v0, /device:TPU:0, one launch (start us, length us, event | category | flops | bytes accessed | tf_op | source)
XLA Modules:
  0.0 262.5 jit_solution(222382831714675305)
XLA Ops:
  0.7 253.5 %block.1 = (f32[128,512]{1,0:T(8,128)}, f32[128,512]{1,0:T(8,128)}, f32[128,2048]{1,0:T(8,128)}, f32[128,2048]{1,0:T(8,128)}, f32[128,128]{1,0:T(8,128)}, /*inde...) custom-call(bf16[128,512]{1,0:T(8,128)(2,1)} %x_ref.1, bf16[128,512]{1,0:T(8,128)(2,1)} %cot_ref.1, ...), custom_call_target="tpu_custom_call" | custom-call | tf_op jit(solution)/shard_map/block/pallas_call | solution.py:1472
  254.2 8.2 %adamw.1 = (f32[128,512]{1,0:T(8,128)}, f32[128,512]{1,0:T(8,128)}, f32[5,512]{1,0:T(8,128)}, f32[5,512]{1,0:T(8,128)}, f32[5,512]{1,0:T(8,128)}, /*index=5*/f32...) custom-call(f32[128,512]{1,0:T(8,128)} %get-tuple-element.54.refs_0_, ...), custom_call_target="tpu_custom_call" | custom-call | tf_op jit(solution)/shard_map/adamw/pallas_call | solution.py:1552
where the time goes:
time: 263 us
  Pallas kernels  262 us (100%)
    pallas_call x1, Pallas kernels, per_device(): pl.pallas_call(functools.partial(block_kernel, n_exp, n_dp, n_act, cap),...  254 us
    pallas_call x1, Pallas kernels, per_device(): pl.pallas_call(adam_kernel, grid=(steps,), out_shape=outs, in_specs=[by_r...  8.17 us

commit v1 on v0

--- a/solution.py
+++ b/solution.py
@@ -146,13 +146,15 @@
     mgrad,
     total,
     total_two,
-    pair_send,
+    g_blocks,
+    g_pair_recv,
+    g_far_recv,
+    g_total,
+    blocks_one,
     pair_recv,
-    far_send,
     far_recv,
-    pair_send_two,
+    blocks_two,
     pair_recv_two,
-    far_send_two,
     far_recv_two,
     dkv_send,
     dkv_recv,
@@ -163,9 +165,8 @@
     a_total,
     a_stage,
     a_recv,
-    s_pair_send,
+    s_blocks,
     s_pair_recv,
-    s_far_send,
     s_far_recv,
     s_total,
     s_dp,
@@ -192,6 +193,7 @@
     kg_send,
     kg_recv,
     rs_sems,
+    g_sems,
     rs_sems_two,
     s_sems,
     a_sems,
@@ -258,150 +260,160 @@
         return [lax.rem(low + k, n_low) for k in range(1, n_low)]
 
     class Gather:
-        def __init__(self, buf, send, recv, count):
+        def __init__(self, buf, send, recv, count, parts=1):
             self.buf, self.sent, self.got, self.count = buf, send, recv, count
-
-        def copy(self, block, sem, where):
+            self.parts, self.rows = parts, buf.shape[1] // parts
+
+        def copy(self, block, sem, where, part):
             ref = self.buf.at[block]
-            return remote(ref, ref, self.sent.at[sem], self.got.at[block], expert=where)
+            if self.parts > 1:
+                ref = self.buf.at[block, pl.ds(part * self.rows, self.rows)]
+            return remote(
+                ref, ref, self.sent.at[part, sem], self.got.at[part, block], expert=where
+            )
 
         def start(self):
-            for k in (*range(1, pairs, 2), *range(2, pairs, 2)):
-                self.send(k)
-            self.send(0)
-
-        def send(self, k):
+            for part in range(self.parts):
+                self.start_part(part)
+
+        def start_part(self, part):
+            for k in (*range(pairs - 1, 0, -2), *range(pairs - 2, 0, -2)):
+                self.send(k, part)
+            self.send(0, part)
+
+        def send(self, k, part=0):
             zz = lax.rem(chip + k, pairs)
 
             @pl.when(me < self.count)
             def _():
-                self.copy(me, zz, 2 * zz + core if k else sibling).start()
+                self.copy(me, zz, 2 * zz + core if k else sibling, part).start()
 
         def finish(self):
-            for k in range(pairs - 1, 0, -1):
-                zz = lax.rem(chip + k, pairs)
-                src = 2 * zz + core
-
-                @pl.when(src < self.count)
+            for part in range(self.parts):
+                for k in (*range(1, pairs, 2), *range(2, pairs, 2)):
+                    zz = lax.rem(chip + k, pairs)
+                    src = 2 * zz + core
+
+                    @pl.when(src < self.count)
+                    def _():
+                        self.copy(src, zz, src, part).wait_recv()
+                        self.copy(src, pairs + zz, sibling, part).start()
+
+            for part in range(self.parts):
+                for k in range(pairs):
+                    zz = lax.rem(chip + k, pairs)
+                    src = 2 * zz + 1 - core
+
+                    @pl.when(src < self.count)
+                    def _():
+                        self.copy(src, zz, sibling, part).wait_recv()
+
+            for part in range(self.parts):
+
+                @pl.when(me < self.count)
                 def _():
-                    self.copy(src, zz, src).wait_recv()
-                    self.copy(src, pairs + zz, sibling).start()
-
-            for k in range(pairs):
-                zz = lax.rem(chip + k, pairs)
-                src = 2 * zz + 1 - core
-
-                @pl.when(src < self.count)
-                def _():
-                    self.copy(src, zz, sibling).wait_recv()
-
-            @pl.when(me < self.count)
-            def _():
+                    for k in range(1, pairs):
+                        zz = lax.rem(chip + k, pairs)
+                        self.copy(me, zz, 2 * zz + core, part).wait_send()
+                    self.copy(me, chip, sibling, part).wait_send()
+
                 for k in range(1, pairs):
                     zz = lax.rem(chip + k, pairs)
-                    self.copy(me, zz, 2 * zz + core).wait_send()
-                self.copy(me, chip, sibling).wait_send()
-
-            for k in range(1, pairs):
-                zz = lax.rem(chip + k, pairs)
-                src = 2 * zz + core
-
-                @pl.when(src < self.count)
-                def _():
-                    self.copy(src, pairs + zz, sibling).wait_send()
+                    src = 2 * zz + core
+
+                    @pl.when(src < self.count)
+                    def _():
+                        self.copy(src, pairs + zz, sibling, part).wait_send()
 
     class Reduce:
-        def __init__(self, count, rows, psend, precv, fsend, frecv, sems, result, halves=False):
-            self.halves = halves
+        def __init__(self, count, cuts, blocks, precv, frecv, sems, result):
+            rows = sum(cuts)
             self.count, self.rows, self.part = count, rows, pl.ds(0, rows)
-            self.psend, self.precv, self.fsend, self.frecv = psend, precv, fsend, frecv
+            self.cuts = [pl.ds(sum(cuts[:at]), size) for at, size in enumerate(cuts)]
+            self.blocks, self.precv, self.frecv = blocks, precv, frecv
             self.sems, self.result = sems, result
 
         def pair_copy(self, zz):
             return remote(
-                self.psend.at[zz, self.part],
+                self.blocks.at[2 * zz + 1 - core, self.part],
                 self.precv.at[zz, self.part],
                 self.sems.at[0, zz],
                 self.sems.at[1, zz],
                 expert=sibling,
             )
 
-        def far_copy(self, zz, slot, half=None):
-            part = self.part if half is None else pl.ds(half * (self.rows // 2), self.rows // 2)
-            at = 2 if half is None else 2 + 2 * half
+        def far_copy(self, zz, slot, part):
             return remote(
-                self.fsend.at[zz, part],
-                self.frecv.at[slot, part],
-                self.sems.at[at, zz],
-                self.sems.at[at + 1, slot],
+                self.blocks.at[2 * zz + core, self.cuts[part]],
+                self.frecv.at[slot, self.cuts[part]],
+                self.sems.at[2 + 2 * part, zz],
+                self.sems.at[3 + 2 * part, slot],
                 expert=2 * zz + core,
             )
 
-        def far_parts(self):
-            return (0, 1) if self.halves else (None,)
-
-        def far_copies(self, zz, slot):
-            return [self.far_copy(zz, slot, half) for half in self.far_parts()]
-
-        def start(self, make, send):
-            for k in range(pairs):
-                zz = lax.rem(chip + 1 + k, pairs)
-                block = 2 * zz + 1 - core
+        def start(self, send):
+            self.start_pairs()
+            self.start_far(send)
+
+        def start_pairs(self):
+            for k in (*range(pairs - 1, 0, -1), 0):
+                zz = lax.rem(chip + k, pairs)
+
+                @pl.when(2 * zz + 1 - core < self.count)
+                def _():
+                    self.pair_copy(zz).start()
+
+        def start_far(self, send):
+            for k in range(pairs - 1, 0, -1):
+                zz = lax.rem(chip + k, pairs)
+                block = 2 * zz + core
 
                 @pl.when(block < self.count)
                 def _():
-                    self.psend[zz, self.part] = make(block).astype(BF16)
-                    self.pair_copy(zz).start()
-
-            for k in range(1, pairs):
-                zz = lax.rem(chip + k, pairs)
-                block = 2 * zz + core
-
-                @pl.when(block < self.count)
-                def _():
-                    mine = make(block)
                     self.pair_copy(zz).wait_recv()
-                    self.fsend[zz, self.part] = (
-                        mine + self.precv[zz, self.part].astype(F32)
-                    ).astype(BF16)
-
-                    def go():
-                        for copy in self.far_copies(zz, chip):
-                            copy.start()
-
-                    if isinstance(send, bool):
-                        if send:
-                            go()
-                    else:
-                        pl.when(send)(go)
+                    for part, cut in enumerate(self.cuts):
+                        self.blocks[block, cut] = (
+                            self.blocks[block, cut].astype(F32) + self.precv[zz, cut].astype(F32)
+                        ).astype(BF16)
+                        if isinstance(send, bool):
+                            if send:
+                                self.far_copy(zz, chip, part).start()
+                        else:
+                            pl.when(send)(self.far_copy(zz, chip, part).start)
 
             @pl.when(me < self.count)
             def _():
-                mine = make(me)
                 self.pair_copy(chip).wait_recv()
-                self.result[self.part] = mine + self.precv[chip, self.part].astype(F32)
+                self.result[self.part] = self.blocks[me, self.part].astype(F32) + self.precv[
+                    chip, self.part
+                ].astype(F32)
 
             @pl.when(me >= self.count)
             def _():
                 self.result[self.part] = jnp.zeros((self.rows, self.result.shape[1]), F32)
 
         def send(self, *parts):
-            for k, half in parts:
+            for k, part in parts:
                 zz = lax.rem(chip + k, pairs)
 
                 @pl.when(2 * zz + core < self.count)
                 def _():
-                    self.far_copy(zz, chip, self.far_parts()[half]).start()
+                    self.far_copy(zz, chip, part).start()
 
         def finish(self):
+            for part in range(len(self.cuts)):
+                self.finish_part(part)
+            self.finish_sends()
+
+        def finish_part(self, part):
             @pl.when(me < self.count)
             def _():
                 for k in range(1, pairs):
                     zz = lax.rem(chip + k, pairs)
-                    for copy in self.far_copies(zz, zz):
-                        copy.wait_recv()
-                    self.result[self.part] += self.frecv[zz, self.part].astype(F32)
-
+                    self.far_copy(zz, zz, part).wait_recv()
+                    self.result[self.cuts[part]] += self.frecv[zz, self.cuts[part]].astype(F32)
+
+        def finish_sends(self):
             for k in range(pairs):
                 zz = lax.rem(chip + 1 + k, pairs)
 
@@ -414,8 +426,8 @@
 
                 @pl.when(2 * zz + core < self.count)
                 def _():
-                    for copy in self.far_copies(zz, chip):
-                        copy.wait_send()
+                    for part in range(len(self.cuts)):
+                        self.far_copy(zz, chip, part).wait_send()
 
     def attn_weight_copy(peer, slot):
         ref = w_all.at[me, shard_rows(slot)]
@@ -612,6 +624,8 @@
         for peer in low_peers():
             down_low(peer, low, block).start()
 
+    rows_gather = Gather(rows_all.at[0], ag_send, ag_recv, n_act)
+
     def attention(loop):
         normed = normed_k[loop]
 
@@ -664,7 +678,6 @@
         second_k[loop] = second
         rows_all[0, me] = second
 
-    rows_gather = Gather(rows_all.at[0], ag_send, ag_recv, n_act)
     factor_gather = Gather(wrow, fg_send, fg_recv, n_act)
 
     def place_matrices(loop):
@@ -681,8 +694,9 @@
 
         lax.fori_loop(0, n_act, block_matrix, 0)
 
-    def scatter_rows(block):
-        return scatter_m[pl.ds(pl.multiple_of(block * own, own), own)]
+    def spread_rows(blocks, terms):
+        rows = nn(scatter_m[...], terms).astype(BF16)
+        blocks[0:n_act] = rows.reshape(n_act, own, width)
 
     def take(buf):
         return nn(gather_m[...], rows_all[buf, 0:n_act].reshape(valid_rows, width))
@@ -722,22 +736,22 @@
 
     sums = Reduce(
         n_act,
-        own,
-        pair_send_two,
+        [own // 2, own // 2],
+        blocks_two,
         pair_recv_two,
-        far_send_two,
         far_recv_two,
         rs_sems_two,
         total_two,
-        True,
     )
     back_sums = Reduce(
-        n_act, own + EXTRA, pair_send, pair_recv, far_send, far_recv, rs_sems, total
+        n_act, [own // 2, own // 2], blocks_one, pair_recv, far_recv, rs_sems, total
     )
+    gate_sums = Reduce(n_act, [EXTRA], g_blocks, g_pair_recv, g_far_recv, g_sems, g_total)
 
     def start_terms(loop, send):
         terms = (part_k[cap_rows(loop)] * fgate_k[cap_rows(loop)]).astype(BF16)
-        sums.start(lambda block: nn(scatter_rows(block), terms), send)
+        spread_rows(blocks_two, terms)
+        sums.start(send)
 
     def wait_weights():
         for peer in high_peers():
@@ -821,18 +835,14 @@
         )
         spread_t = jnp.transpose(spread)[0:EXTRA].astype(BF16)
 
-        def row_terms(block):
-            matrix = scatter_rows(block)
-            grads = nt(spread_t, matrix)
-            return jnp.concatenate(
-                [
-                    nn(matrix, terms),
-                    jnp.concatenate([grads, jnp.zeros((EXTRA, width - own), F32)], axis=1),
-                ],
-                axis=0,
-            )
-
-        back_sums.start(row_terms, True)
+        grads = nt(spread_t, scatter_m[...]).astype(BF16)
+        for block in range(n_act):
+            g_blocks[block] = grads[:, block * own : (block + 1) * own]
+        gate_sums.start_pairs()
+        spread_rows(blocks_one, terms)
+        back_sums.start_pairs()
+        gate_sums.start_far(True)
+        back_sums.start_far(True)
 
     def expert_weights(loop):
         rows_in = rows_k[cap_rows(loop)]
@@ -941,10 +951,9 @@
 
     attn_sums = Reduce(
         n_exp,
-        2 * HD,
-        pair_send_two,
+        [2 * HD],
+        blocks_two,
         pair_recv_two,
-        far_send_two,
         far_recv_two,
         a_sems,
         total_two,
@@ -963,8 +972,8 @@
         info = meta_ref[loop, own_rows, 0 : 2 * n_exp]
         running = running_rows(loop)
         branch = (sgrad[loop] + carry[...]) * running
-        second_grad = total[0:own]
-        gate_rows = total[own : own + n_exp, 0:own] + total[own + n_exp : own + 2 * n_exp, 0:own]
+        gate_sums.finish_part(0)
+        gate_rows = g_total[0:n_exp] + g_total[n_exp : 2 * n_exp]
         gate_rows = jnp.concatenate(
             [jnp.zeros((n_exp, own), F32), gate_rows, jnp.zeros((LANES - 2 * n_exp, own), F32)],
             axis=0,
@@ -974,35 +983,43 @@
         gates = masked_softmax(nt(second, rb[...]), (info > 0.5) & (route_lane >= n_exp))
         loop_dot = jnp.sum(gates * gate_grads, axis=1, keepdims=True)
         logit_grad = (gates * (gate_grads - loop_dot)).astype(BF16)
-        second_grad = second_grad + nn(logit_grad, rb[...])
-        unit, inverse = normalise(middle[loop])
-        middle_grad = norm_back(second_grad, unit, inverse, gain_two) + branch
-        mgrad[...] = middle_grad
-
+        router_part = nn(logit_grad, rb[...])
         gates = gate_k[loop]
         kv_rows = window_keys(loop)
-        dkv_t[...] = jnp.zeros_like(dkv_t)
-
-        def scores_back(pair, none):
-            rows = pl.ds(pl.multiple_of(pair * 2 * own, 2 * own), 2 * own)
-            out_grads = []
-            for half in range(2):
-                expert = 2 * pair + half
-                part_grad = (column(gates, expert, route_lane) * mgrad[...]).astype(BF16)
-                out_grads.append(
-                    jnp.where(lane < HD, 0.0, nn(part_grad, w_all[expert])).astype(BF16)
-                )
-            out_grad = jnp.concatenate(out_grads, axis=0)
-            prob_low = p_k[loop, rows]
-            prob = prob_low.astype(F32)
-            prob_grad = nt(out_grad, kv_rows)
-            centre = jnp.sum(prob * prob_grad, axis=1, keepdims=True)
-            score_grad = (prob * (prob_grad - centre)).astype(BF16)
-            ds_k[rows] = score_grad
-            dkv_t[...] += tn(q_k[loop, rows], score_grad) * scale + tn(out_grad, prob_low)
-            return none
-
-        lax.fori_loop(0, n_exp // 2, scores_back, 0, unroll=True)
+        half = own // 2
+
+        for part in range(2):
+            at = part * half
+            back_sums.finish_part(part)
+            second_grad = total[at : at + half] + router_part[at : at + half]
+            total[at : at + half] = second_grad
+            unit, inverse = normalise(middle[loop, at : at + half])
+            middle_grad = norm_back(second_grad, unit, inverse, gain_two) + branch[at : at + half]
+            mgrad[at : at + half] = middle_grad
+            for quad in range(n_exp // 4):
+                experts = range(4 * quad, 4 * quad + 4)
+                out_grads = []
+                for expert in experts:
+                    part_grad = (gates[at : at + half, expert : expert + 1] * middle_grad).astype(
+                        BF16
+                    )
+                    out_grads.append(nn(part_grad, w_all[expert]))
+                out_grad = jnp.concatenate(out_grads, axis=0)
+                out_grad = jnp.where(lane_two < HD, 0.0, out_grad).astype(BF16)
+                rows = [slice(e * own + at, e * own + at + half) for e in experts]
+                prob_low = jnp.concatenate([p_k[loop, cut] for cut in rows], axis=0)
+                query = jnp.concatenate([q_k[loop, cut] for cut in rows], axis=0)
+                prob = prob_low.astype(F32)
+                prob_grad = nt(out_grad, kv_rows)
+                centre = jnp.sum(prob * prob_grad, axis=1, keepdims=True)
+                score_grad = (prob * (prob_grad - centre)).astype(BF16)
+                for index, cut in enumerate(rows):
+                    ds_k[cut] = score_grad[index * half : (index + 1) * half]
+                grads = tn(query, score_grad) * scale + tn(out_grad, prob_low)
+                if part or quad:
+                    dkv_t[...] += grads
+                else:
+                    dkv_t[...] = grads
         for block in range(window):
             grads = jnp.transpose(dkv_t[:, block * own : (block + 1) * own])
             dkv[block] = grads
@@ -1013,6 +1030,8 @@
             def _():
                 dkv_copy(distance, me - distance).start()
 
+        back_sums.finish_sends()
+        gate_sums.finish_sends()
         @pl.when(step == last)
         def _():
             state_grads(loop_dot)
@@ -1023,6 +1042,8 @@
             sums.send((3, 1))
 
         small_acc[2 * HD : vec_at] += tn(logit_grad, second)
+        second_grad = total[...]
+        unit, _ = normalise(middle[loop])
         small_acc[vec_at + 2 : vec_at + 3] += jnp.sum(second_grad * unit, axis=0, keepdims=True)
         small_acc[vec_at + 3 : vec_at + 4] += jnp.sum(second_grad, axis=0, keepdims=True)
         normed = normed_k[loop]
@@ -1048,7 +1069,8 @@
 
         @pl.when(loop == 0)
         def _():
-            attn_sums.start(lambda block: attn_acc[block], False)
+            blocks_two[...] = attn_acc[...].astype(BF16)
+            attn_sums.start(False)
 
         gate_grads = dga[...]
         logit_grad = (
@@ -1177,7 +1199,6 @@
             def _():
                 send_expert_weights()
 
-            back_sums.finish()
 
             @pl.when(step == last)
             def _():
@@ -1196,11 +1217,10 @@
 
     chunk = small_acc.shape[0] // n_exp
     small_sums = Reduce(
-        n_exp, chunk, s_pair_send, s_pair_recv, s_far_send, s_far_recv, s_sems, s_total
+        n_exp, [chunk], s_blocks, s_pair_recv, s_far_recv, s_sems, s_total
     )
-    small_sums.start(
-        lambda block: small_acc[pl.ds(pl.multiple_of(block * chunk, chunk), chunk)], True
-    )
+    s_blocks[...] = small_acc[...].astype(BF16).reshape(n_exp, chunk, width)
+    small_sums.start(True)
     attn_sums.send((1, 0), (3, 0), (2, 0))
 
     def attn_copy(peer, slot):
@@ -1356,7 +1376,7 @@
     small_rows = 32 * n_exp
     vmem = pltpu.VMEM
     dma = pltpu.SemaphoreType.DMA
-    block = (pairs, own + EXTRA, width)
+    block = (pairs, own, width)
     small_block = (pairs, 32, width)
     scratch = [
         vmem((LOOPS, slots, INFO), F32),
@@ -1401,14 +1421,16 @@
         vmem((LOOPS, own, width), F32),
         vmem((own, width), F32),
         vmem((own, width), F32),
-        vmem((own + EXTRA, width), F32),
         vmem((own, width), F32),
+        vmem((own, width), F32),
+        vmem((n_exp, EXTRA, own), BF16),
+        vmem((pairs, EXTRA, own), BF16),
+        vmem((pairs, EXTRA, own), BF16),
+        vmem((EXTRA, own), F32),
+        vmem((n_exp, own, width), BF16),
         vmem(block, BF16),
         vmem(block, BF16),
-        vmem(block, BF16),
-        vmem(block, BF16),
-        vmem((pairs, own, width), BF16),
-        vmem((pairs, own, width), BF16),
+        vmem((n_exp, own, width), BF16),
         vmem((pairs, own, width), BF16),
         vmem((pairs, own, width), BF16),
         vmem((window, own, 2 * HD), BF16),
@@ -1420,8 +1442,7 @@
         vmem((width, 2 * HD), F32),
         vmem((width, 2 * HD), BF16),
         vmem((width, 2 * HD), BF16),
-        vmem(small_block, BF16),
-        vmem(small_block, BF16),
+        vmem((n_exp, 32, width), BF16),
         vmem(small_block, BF16),
         vmem(small_block, BF16),
         vmem((32, width), F32),
@@ -1436,18 +1457,19 @@
         dma((n_high,)),
         dma((n_dp,)),
         dma((n_low, n_high)),
-        dma((2 * pairs,)),
-        dma((n_exp,)),
-        dma((2 * pairs,)),
-        dma((n_exp,)),
-        dma((2 * pairs,)),
-        dma((n_exp,)),
-        dma((2 * pairs,)),
-        dma((n_exp,)),
-        dma((2 * pairs,)),
-        dma((n_exp,)),
+        dma((1, 2 * pairs)),
+        dma((1, n_exp)),
+        dma((1, 2 * pairs)),
+        dma((1, n_exp)),
+        dma((1, 2 * pairs)),
+        dma((1, n_exp)),
+        dma((1, 2 * pairs)),
+        dma((1, n_exp)),
+        dma((1, 2 * pairs)),
+        dma((1, n_exp)),
         dma((window,)),
         dma((n_exp,)),
+        dma((6, pairs)),
         dma((4, pairs)),
         dma((6, pairs)),
         dma((4, pairs)),

time: 263 us -> 256 us (0.973)
  Pallas kernels: 262 us -> 255 us
    pallas_call x1, Pallas kernels: 254 us -> 247 us  [per_device(): pl.pallas_call(functools.partial(block_kernel, n_exp, n_dp, n_act, cap),...]
where the time goes in v1:
time: 256 us
  Pallas kernels  255 us (100%)
    pallas_call x1, Pallas kernels, per_device(): pl.pallas_call(functools.partial(block_kernel, n_exp, n_dp, n_act, cap),...  247 us
    pallas_call x1, Pallas kernels, per_device(): pl.pallas_call(adam_kernel, grid=(steps,), out_shape=outs, in_specs=[by_r...  8.17 us

profile of v1, /device:TPU:0, one launch (start us, length us, event | category | flops | bytes accessed | tf_op | source)
XLA Modules:
  0.0 255.8 jit_solution(5616896386383792660)
XLA Ops:
  0.7 246.8 %block.1 = (f32[128,512]{1,0:T(8,128)}, f32[128,512]{1,0:T(8,128)}, f32[128,2048]{1,0:T(8,128)}, f32[128,2048]{1,0:T(8,128)}, f32[128,128]{1,0:T(8,128)}, /*inde...) custom-call(bf16[128,512]{1,0:T(8,128)(2,1)} %x_ref.1, bf16[128,512]{1,0:T(8,128)(2,1)} %cot_ref.1, ...), custom_call_target="tpu_custom_call" | custom-call | tf_op jit(solution)/shard_map/block/pallas_call | solution.py:1494
  247.5 8.2 %adamw.1 = (f32[128,512]{1,0:T(8,128)}, f32[128,512]{1,0:T(8,128)}, f32[5,512]{1,0:T(8,128)}, f32[5,512]{1,0:T(8,128)}, f32[5,512]{1,0:T(8,128)}, /*index=5*/f32...) custom-call(f32[128,512]{1,0:T(8,128)} %get-tuple-element.54.refs_0_, ...), custom_call_target="tpu_custom_call" | custom-call | tf_op jit(solution)/shard_map/adamw/pallas_call | solution.py:1574
